TPU v7x, 512 devices: a whole 4x4x16 slice. The times are simulated.
512 devices in a mesh: row: 32 (over z, y_hi), col: 16 (over x, y_lo, core).
Axes of the slice: x: 4, y: 4 (y_hi: 2, y_lo: 2; y = y_hi * 2 + y_lo), z: 16, core: 2. Of those that a mesh axis runs over, the one named last changes fastest.
Arguments:
- blocks: float32 [32, 16, 8, 128, 128], P('row', 'col'), may hold values from -1.2 to 1.2
- block_rows: int32 [32, 16, 8], P('row', 'col'), may hold values from -1 to 15, as said below
- block_cols: int32 [32, 16, 8], P('row', 'col'), may hold values from -1 to 31, as said below
Outputs:
- square_part: float32 [32, 16, 8, 128, 128], P('row', 'col')
Inputs may be any that keep to these rules, and one draw needn't show every extreme that they name: Empty slots have -1 in block_rows and block_cols alike; a used slot has a block row below 16; no block is listed twice in one tile. At most 4 used slots of one tile share a block row, and some tile has a block row with exactly 4. Some tile uses all 8 slots, and some tile has empty slots. `block_cols`: the two lists describe the same slots; a used slot has a block column below 32.
All inputs are finite; a program needn't handle non-finite values.
Results may differ from a plain program's by a relative error of at most 0.0003.
Values sent between devices are 32-bit elements; how exact they have to be, the bound alone decides.
A program may use at most 64 MiB of HBM per device.

v0:
```python
import jax
import jax.numpy as jnp
from jax import lax
from jax.sharding import PartitionSpec as P

NBLK = 512
ACT = 2
SECTIONS = 4


def from_root(x, axis, root):
    mine = lax.axis_index(axis) == root
    return lax.psum(jnp.where(mine, x, jnp.zeros_like(x)), axis)


def from_partner(x, axis, bit):
    return lax.ppermute(x, axis, [(i, i ^ 1 << bit) for i in range(lax.axis_size(axis))])


def shifted(value, axis, steps):
    count = lax.axis_size(axis)
    pairs = [(source, (source + steps) % count) for source in range(count)]
    return lax.ppermute(value, axis, pairs)


def section_product(panel, pair, out_rows, out_cols, depth):
    panel_vals, panel_rows, panel_cols = panel
    pair_vals, pair_inner, pair_cols = pair
    panel_iota = jnp.arange(panel_rows.shape[0], dtype=jnp.int32)
    pair_iota = jnp.arange(pair_inner.shape[0], dtype=jnp.int32)
    depth_iota = jnp.arange(depth, dtype=jnp.int32)
    panel_live = panel_rows >= 0
    earlier = (
        (panel_rows[None, :] == panel_rows[:, None])
        & panel_live[None, :]
        & (panel_iota[None, :] < panel_iota[:, None])
    )
    within = jnp.sum(earlier.astype(jnp.int32), axis=1)
    picked = (panel_rows[None, None, :] == out_rows[:, None, None]) & (
        within[None, None, :] == depth_iota[None, :, None]
    )
    picked = picked & panel_live[None, None, :] & (out_rows >= 0)[:, None, None]
    picked_int = picked.astype(jnp.int32)
    panel_slot = jnp.sum(picked_int * panel_iota[None, None, :], axis=2)
    found = jnp.sum(picked_int, axis=2) > 0
    inner = jnp.sum(picked_int * panel_cols[None, None, :], axis=2)
    matched = (pair_inner[None, None, :] == inner[:, :, None]) & (
        pair_cols[None, None, :] == out_cols[:, None, None]
    )
    matched = matched & (pair_inner >= 0)[None, None, :] & found[:, :, None]
    matched_int = matched.astype(jnp.int32)
    pair_slot = jnp.sum(matched_int * pair_iota[None, None, :], axis=2)
    weight = (jnp.sum(matched_int, axis=2) > 0).astype(jnp.float32)
    left = panel_vals[panel_slot] * weight[:, :, None, None]
    right = pair_vals[pair_slot]
    return jnp.einsum(
        "tqij,tqjk->tik",
        left,
        right,
        precision=lax.Precision.HIGHEST,
        preferred_element_type=jnp.float32,
    )


def make_pair(first, second, row_span):
    inner = jnp.concatenate([first[1], jnp.where(second[1] >= 0, second[1] + row_span, -1)])
    return (jnp.concatenate([first[0], second[0]]), inner, jnp.concatenate([first[2], second[2]]))


def order_pair(mine, other, is_even, row_span):
    first = tuple((jnp.where(is_even, one, two) for one, two in zip(mine, other)))
    second = tuple((jnp.where(is_even, two, one) for one, two in zip(mine, other)))
    return make_pair(first, second, row_span)


def fetch_panel(tile, row_index, col_count, section):
    root = (row_index // 2 + section) % col_count
    return (
        from_root(tile[0], "col", root),
        from_root(tile[1], "col", root),
        from_root(tile[2], "col", root),
    )


def body(blocks, block_rows, block_cols):
    tile = (blocks[0, 0], block_rows[0, 0], block_cols[0, 0])
    row_count = lax.axis_size("row")
    col_count = lax.axis_size("col")
    row_span = NBLK // row_count
    row_index = lax.axis_index("row")
    is_even = row_index % 2 == 0
    depth = 2 * ACT
    total = jnp.zeros(blocks.shape[2:], jnp.float32)
    partner = from_partner((tile[0], tile[1], tile[2]), "row", 0)
    start_pair = order_pair(tile, partner, is_even, row_span)
    current = start_pair
    for section in range(SECTIONS):
        panel = fetch_panel(tile, row_index, col_count, section)
        if section > 0:
            current = shifted((current[0], current[1], current[2]), "row", -2)
        total = total + section_product(panel, current, tile[1], tile[2], depth)
    return total[None, None]


def solution(mesh):
    return jax.shard_map(
        body,
        mesh=mesh,
        in_specs=(P("row", "col", None, None, None), P("row", "col", None), P("row", "col", None)),
        out_specs=P("row", "col", None, None, None),
        check_vma=False,
    )
```

profile of v0, /device:TPU:1, one launch (start us, length us, event | category | flops | bytes accessed | tf_op | source)
XLA Modules:
  0.0 244.3 jit_solution(5052952195378283427)
XLA Ops:
  6.5 5.6 %collective-permute-start.2 = (f32[8,128,128]{2,1,0:T(8,128)}, f32[8,128,128]{2,1,0:T(8,128)S(1)}, u32[]{:S(2)}, u32[]{:S(2)}) collective-permute-start(f32[8,128,128]{2,1,0:T(8,128)} %bitcast.96), channel_id=1, source_target_pairs={{0,16},{16,0},{32,48},{48,32},{64,80},{80,64},{96,112},{112,96},{1... | collective-permute-start | bytes 1572872 | tf_op jit(solution)/shard_map/ppermute | solution.py:17
  12.2 1.9 collective-permute-start
  14.1 4.9 %collective-permute-start.1 = (s32[8]{0:T(128)}, s32[8]{0:T(128)S(1)}, u32[]{:S(2)}, u32[]{:S(2)}) collective-permute-start(s32[8]{0:T(128)} %bitcast.99), channel_id=1, source_target_pairs={{0,16},{16,0},{32,48},{48,32},{64,80},{80,64},{96,112},{112,96},{1... | collective-permute-start | bytes 104 | tf_op jit(solution)/shard_map/ppermute | solution.py:17
  19.1 0.7 broadcast_compare_fusion.19
  19.7 1.1 collective-permute-done
  20.8 0.7 broadcast_select_fusion.15
  21.5 0.7 broadcast_select_fusion.13
  22.2 13.9 %all-reduce = (s32[8]{0:T(128)S(1)}, s32[8]{0:T(128)S(1)}, s32[8]{0:T(128)S(1)}, s32[8]{0:T(128)S(1)}, s32[8]{0:T(128)S(1)}, /*index=5*/s32[8]{0:T(128)S(1)}, s32[8]{0:T(128)S(1)}, s32[8]{0:T(128)S(1)}) all-reduce(s32[8]{0:T(128)S(1)} %get-tuple-element.71, s32[8]{0:T(128)S(1)} %get-tuple-element.67, ...), channel_id=1, replica_groups=mesh['row'=32,'col'=16] {'col'}, use_global_device_ids=true, to_apply=%region_28.29 | all-reduce | flops 64 | bytes 512 | tf_op jit(solution)/shard_map/psum | solution.py:13
  36.0 0.7 broadcast_compare_fusion.7
  36.8 0.2 convert_reduce_fusion.8
  37.0 0.2 convert_reduce_fusion.10
  37.3 1.0 select_reduce_fusion.2
  38.3 11.1 %collective-permute-start.4 = (s32[16]{0:T(128)S(1)}, s32[16]{0:T(128)S(1)}, u32[]{:S(2)}, u32[]{:S(2)}) collective-permute-start(s32[16]{0:T(128)S(1)} %pad_add_fusion.1), channel_id=1, source_target_pairs={{0,480},{16,496},{32,0},{48,16},{64,32},{80,48},{96,64},{112,80},{... | collective-permute-start | bytes 200 | tf_op jit(solution)/shard_map/ppermute | solution.py:23
  49.5 0.1 copy.20
  49.5 0.1 reshape.513
  49.6 0.1 broadcast_compare_fusion.15
  49.7 2.6 %collective-permute-start.3 = (s32[16]{0:T(128)S(1)}, s32[16]{0:T(128)S(1)}, u32[]{:S(2)}, u32[]{:S(2)}) collective-permute-start(s32[16]{0:T(128)S(1)} %get-tuple-element.47), channel_id=1, source_target_pairs={{0,480},{16,496},{32,0},{48,16},{64,32},{80,48},{96,64},{112,80},{... | collective-permute-start | bytes 200 | tf_op jit(solution)/shard_map/ppermute | solution.py:23
  52.4 0.1 copy.23
  52.5 0.1 reshape.529
  52.6 0.1 copy.26
  52.7 0.1 reshape.545
  52.8 0.1 copy.29
  52.9 0.1 reshape.561
  53.0 2.6 %collective-permute-start.7 = (s32[16]{0:T(128)S(1)}, s32[16]{0:T(128)S(1)}, u32[]{:S(2)}, u32[]{:S(2)}) collective-permute-start(s32[16]{0:T(128)S(1)} %collective-permute-done.4), channel_id=1, source_target_pairs={{0,480},{16,496},{32,0},{48,16},{64,32},{80,48},{96,64},{112,80},{... | collective-permute-start | bytes 200 | tf_op jit(solution)/shard_map/ppermute | solution.py:23
  55.6 2.6 %collective-permute-start.6 = (s32[16]{0:T(128)S(1)}, s32[16]{0:T(128)S(1)}, u32[]{:S(2)}, u32[]{:S(2)}) collective-permute-start(s32[16]{0:T(128)S(1)} %collective-permute-done.3), channel_id=1, source_target_pairs={{0,480},{16,496},{32,0},{48,16},{64,32},{80,48},{96,64},{112,80},{... | collective-permute-start | bytes 200 | tf_op jit(solution)/shard_map/ppermute | solution.py:23
  58.3 3.8 %collective-permute-start.10 = (s32[16]{0:T(128)S(1)}, s32[16]{0:T(128)S(1)}, u32[]{:S(2)}, u32[]{:S(2)}) collective-permute-start(s32[16]{0:T(128)S(1)} %collective-permute-done.7), channel_id=1, source_target_pairs={{0,480},{16,496},{32,0},{48,16},{64,32},{80,48},{96,64},{112,80},{... | collective-permute-start | bytes 200 | tf_op jit(solution)/shard_map/ppermute | solution.py:23
  62.1 2.6 %collective-permute-start.9 = (s32[16]{0:T(128)S(1)}, s32[16]{0:T(128)S(1)}, u32[]{:S(2)}, u32[]{:S(2)}) collective-permute-start(s32[16]{0:T(128)S(1)} %collective-permute-done.6), channel_id=1, source_target_pairs={{0,480},{16,496},{32,0},{48,16},{64,32},{80,48},{96,64},{112,80},{... | collective-permute-start | bytes 200 | tf_op jit(solution)/shard_map/ppermute | solution.py:23
  64.8 0.7 broadcast_compare_fusion
  65.5 0.3 convert_reduce_fusion.6
  65.9 2.4 broadcast_select_fusion
  68.3 0.1 pad_maximum_fusion
  68.4 2.8 %collective-permute-start.5 = (f32[16,128,128]{2,1,0:T(8,128)S(1)}, f32[16,128,128]{2,1,0:T(8,128)S(1)}, u32[]{:S(2)}, u32[]{:S(2)}) collective-permute-start(f32[16,128,128]{2,1,0:T(8,128)S(1)} %pad_maximum_fusion), channel_id=1, source_target_pairs={{0,480},{16,496},{32,0},{48,16},{64,32},{80,48},{96,64},{112,80},{... | collective-permute-start | bytes 3145736 | tf_op jit(solution)/shard_map/ppermute | solution.py:23
  71.2 0.3 convert_reduce_fusion.4
  71.5 0.1 copy.22
  71.6 0.1 reshape.521
  71.7 0.1 copy.21
  71.8 0.1 copy.25
  71.9 0.1 reshape.537
  72.0 0.1 copy.24
  72.0 0.3 convert_reduce_fusion.2
  72.3 0.1 copy.28
  72.4 0.1 reshape.553
  72.5 0.1 copy.27
  72.6 17.6 %collective-permute-done.5 = f32[16,128,128]{2,1,0:T(8,128)S(1)} collective-permute-done((f32[16,128,128]{2,1,0:T(8,128)S(1)}, f32[16,128,128]{2,1,0:T(8,128)S(1)}, u32[]{:S(2)}, u32[]{:S(2)}) %collective-permute-start.5) | collective-permute-done | bytes 1048608 | tf_op jit(solution)/shard_map/ppermute | solution.py:23
  90.2 3.4 %collective-permute-start.8 = (f32[16,128,128]{2,1,0:T(8,128)S(1)}, f32[16,128,128]{2,1,0:T(8,128)}, u32[]{:S(2)}, u32[]{:S(2)}) collective-permute-start(f32[16,128,128]{2,1,0:T(8,128)S(1)} %collective-permute-done.5), channel_id=1, source_target_pairs={{0,480},{16,496},{32,0},{48,16},{64,32},{80,48},{96,64},{112,80},{... | collective-permute-start | bytes 3145736 | tf_op jit(solution)/shard_map/ppermute | solution.py:23
  93.6 0.3 convert_reduce_fusion
  93.9 0.1 copy.31
  94.0 0.1 reshape.569
  94.1 0.1 copy.30
  94.2 17.7 %collective-permute-done.8 = f32[16,128,128]{2,1,0:T(8,128)} collective-permute-done((f32[16,128,128]{2,1,0:T(8,128)S(1)}, f32[16,128,128]{2,1,0:T(8,128)}, u32[]{:S(2)}, u32[]{:S(2)}) %collective-permute-start.8) | collective-permute-done | bytes 1048608 | tf_op jit(solution)/shard_map/ppermute | solution.py:23
  111.9 3.6 %collective-permute-start.11 = (f32[16,128,128]{2,1,0:T(8,128)}, f32[16,128,128]{2,1,0:T(8,128)}, u32[]{:S(2)}, u32[]{:S(2)}) collective-permute-start(f32[16,128,128]{2,1,0:T(8,128)} %collective-permute-done.8), channel_id=1, source_target_pairs={{0,480},{16,496},{32,0},{48,16},{64,32},{80,48},{96,64},{112,80},{... | collective-permute-start | bytes 3145736 | tf_op jit(solution)/shard_map/ppermute | solution.py:23
  115.5 2.0 gather_fusion.1
  117.5 0.7 gather_fusion.3
  118.2 89.4 %all-reduce.4.cloned.1.call-done = (f32[8,128,128]{2,1,0:T(8,128)}, f32[8,128,128]{2,1,0:T(8,128)}, f32[8,128,128]{2,1,0:T(8,128)}, f32[8,128,128]{2,1,0:T(8,128)}) async-done(((f32[8,128,128]{2,1,0:T(8,128)}, f32[8,128,128]{2,1,0:T(8,128)}, f32[8,128,128]{2,1,0:T(8,128)}, f32[8,128,128]{2,1,0:T(8,128)}), (f32[8,128,128]{2,1,0:T(8,128)}, f32[8,128,128]{2,1,0:T(8,128)}, f32[8,128,128]{2,1,0:T(8,128)}, ...) | async-done | bytes 2097168 | tf_op jit(solution)/shard_map/psum | solution.py:13
  207.6 3.1 %gather_fusion = f32[32,128,128]{2,1,0:T(8,128)} fusion(f32[8,128,128]{2,1,0:T(8,128)} %get-tuple-element.42, s32[1024]{0:T(1024)S(1)} %pad_clamp_fusion.7), kind=kCustom, calls=%fused_computation | custom fusion | bytes 4194432 | tf_op jit(solution)/shard_map/gather | solution.py:54
  210.7 2.0 gather_fusion.2
  212.7 2.1 gather_fusion.4
  214.8 2.0 gather_fusion.6
  216.8 3.2 %gather_fusion.5 = f32[32,128,128]{2,1,0:T(8,128)} fusion(f32[16,128,128]{2,1,0:T(8,128)} %collective-permute-done.8, s32[1024]{0:T(1024)S(1)} %pad_clamp_fusion.2), kind=kCustom, calls=%fused_computation.5 | custom fusion | bytes 4194432 | tf_op jit(solution)/shard_map/gather | solution.py:55
  220.0 4.7 %fusion.8 = f32[8,128,128]{2,1,0:T(8,128)S(1)} fusion(f32[8,4,128,128]{3,2,1,0:T(8,128)} %bitcast.94, f32[8,4,128,128]{3,2,1,0:T(8,128)} %bitcast.95, f32[8,4]{1,0:T(8,128)S(1)} %copy.21), kind=kOutput, calls=%fused_computation.16 | convolution fusion | flops 805830656 | bytes 4718720 | tf_op jit(solution)/shard_map/tqij,tqjk->tik/dot_general | solution.py:56
  224.8 2.4 fusion.29
  227.2 2.3 fusion.26
  229.5 3.4 %gather_fusion.7 = f32[32,128,128]{2,1,0:T(8,128)} fusion(f32[16,128,128]{2,1,0:T(8,128)} %collective-permute-done.11, s32[1024]{0:T(1024)S(1)} %pad_clamp_fusion), kind=kCustom, calls=%fused_computation.7 | custom fusion | bytes 4194432 | tf_op jit(solution)/shard_map/gather | solution.py:55
  232.9 4.6 %fusion.23 = f32[1,1,8,128,128]{4,3,2,1,0:T(8,128)} fusion(f32[8,128,128]{2,1,0:T(8,128)S(1)} %fusion.26, f32[8,4,128,128]{3,2,1,0:T(8,128)} %bitcast.93, f32[8,4,128,128]{3,2,1,0:T(8,128)S(1)} %bitcast.89, f32[8,4]{1,0:T(8,128)S(1)} %copy.30), kind=kOutput, calls=%fused_computation.21 | convolution fusion | flops 805961728 | bytes 5243008 | tf_op jit(solution)/shard_map/tqij,tqjk->tik/dot_general | solution.py:56
  (61 shorter events, 0.4 us)
Async XLA Ops:
  6.5 201.1 %all-reduce.4.cloned.1.call-start = ((), (), s32[]{:S(2)}) async-start(), calls=%async_computation | async-start | bytes 4194304 | tf_op jit(solution)/shard_map/psum | solution.py:13
  6.5 59.3 %collective-permute-start.2 = (f32[8,128,128]{2,1,0:T(8,128)}, f32[8,128,128]{2,1,0:T(8,128)S(1)}, u32[]{:S(2)}, u32[]{:S(2)}) collective-permute-start(f32[8,128,128]{2,1,0:T(8,128)} %bitcast.96), channel_id=1, source_target_pairs={{0,16},{16,0},{32,48},{48,32},{64,80},{80,64},{96,112},{112,96},{1... | collective-permute-start | bytes 1572872 | tf_op jit(solution)/shard_map/ppermute | solution.py:17
  12.2 8.6 %collective-permute-start = (s32[8]{0:T(128)}, s32[8]{0:T(128)S(1)}, u32[]{:S(2)}, u32[]{:S(2)}) collective-permute-start(s32[8]{0:T(128)} %bitcast.97), channel_id=1, source_target_pairs={{0,16},{16,0},{32,48},{48,32},{64,80},{80,64},{96,112},{112,96},{1... | collective-permute-start | bytes 104 | tf_op jit(solution)/shard_map/ppermute | solution.py:17
  14.1 7.4 %collective-permute-start.1 = (s32[8]{0:T(128)}, s32[8]{0:T(128)S(1)}, u32[]{:S(2)}, u32[]{:S(2)}) collective-permute-start(s32[8]{0:T(128)} %bitcast.99), channel_id=1, source_target_pairs={{0,16},{16,0},{32,48},{48,32},{64,80},{80,64},{96,112},{112,96},{1... | collective-permute-start | bytes 104 | tf_op jit(solution)/shard_map/ppermute | solution.py:17
  38.3 14.6 %collective-permute-start.4 = (s32[16]{0:T(128)S(1)}, s32[16]{0:T(128)S(1)}, u32[]{:S(2)}, u32[]{:S(2)}) collective-permute-start(s32[16]{0:T(128)S(1)} %pad_add_fusion.1), channel_id=1, source_target_pairs={{0,480},{16,496},{32,0},{48,16},{64,32},{80,48},{96,64},{112,80},{... | collective-permute-start | bytes 200 | tf_op jit(solution)/shard_map/ppermute | solution.py:23
  49.7 5.9 %collective-permute-start.3 = (s32[16]{0:T(128)S(1)}, s32[16]{0:T(128)S(1)}, u32[]{:S(2)}, u32[]{:S(2)}) collective-permute-start(s32[16]{0:T(128)S(1)} %get-tuple-element.47), channel_id=1, source_target_pairs={{0,480},{16,496},{32,0},{48,16},{64,32},{80,48},{96,64},{112,80},{... | collective-permute-start | bytes 200 | tf_op jit(solution)/shard_map/ppermute | solution.py:23
  53.0 5.3 %collective-permute-start.7 = (s32[16]{0:T(128)S(1)}, s32[16]{0:T(128)S(1)}, u32[]{:S(2)}, u32[]{:S(2)}) collective-permute-start(s32[16]{0:T(128)S(1)} %collective-permute-done.4), channel_id=1, source_target_pairs={{0,480},{16,496},{32,0},{48,16},{64,32},{80,48},{96,64},{112,80},{... | collective-permute-start | bytes 200 | tf_op jit(solution)/shard_map/ppermute | solution.py:23
  55.6 6.5 %collective-permute-start.6 = (s32[16]{0:T(128)S(1)}, s32[16]{0:T(128)S(1)}, u32[]{:S(2)}, u32[]{:S(2)}) collective-permute-start(s32[16]{0:T(128)S(1)} %collective-permute-done.3), channel_id=1, source_target_pairs={{0,480},{16,496},{32,0},{48,16},{64,32},{80,48},{96,64},{112,80},{... | collective-permute-start | bytes 200 | tf_op jit(solution)/shard_map/ppermute | solution.py:23
  58.3 6.5 %collective-permute-start.10 = (s32[16]{0:T(128)S(1)}, s32[16]{0:T(128)S(1)}, u32[]{:S(2)}, u32[]{:S(2)}) collective-permute-start(s32[16]{0:T(128)S(1)} %collective-permute-done.7), channel_id=1, source_target_pairs={{0,480},{16,496},{32,0},{48,16},{64,32},{80,48},{96,64},{112,80},{... | collective-permute-start | bytes 200 | tf_op jit(solution)/shard_map/ppermute | solution.py:23
  62.1 31.4 %collective-permute-start.9 = (s32[16]{0:T(128)S(1)}, s32[16]{0:T(128)S(1)}, u32[]{:S(2)}, u32[]{:S(2)}) collective-permute-start(s32[16]{0:T(128)S(1)} %collective-permute-done.6), channel_id=1, source_target_pairs={{0,480},{16,496},{32,0},{48,16},{64,32},{80,48},{96,64},{112,80},{... | collective-permute-start | bytes 200 | tf_op jit(solution)/shard_map/ppermute | solution.py:23
  68.4 21.8 %collective-permute-start.5 = (f32[16,128,128]{2,1,0:T(8,128)S(1)}, f32[16,128,128]{2,1,0:T(8,128)S(1)}, u32[]{:S(2)}, u32[]{:S(2)}) collective-permute-start(f32[16,128,128]{2,1,0:T(8,128)S(1)} %pad_maximum_fusion), channel_id=1, source_target_pairs={{0,480},{16,496},{32,0},{48,16},{64,32},{80,48},{96,64},{112,80},{... | collective-permute-start | bytes 3145736 | tf_op jit(solution)/shard_map/ppermute | solution.py:23
  90.2 21.7 %collective-permute-start.8 = (f32[16,128,128]{2,1,0:T(8,128)S(1)}, f32[16,128,128]{2,1,0:T(8,128)}, u32[]{:S(2)}, u32[]{:S(2)}) collective-permute-start(f32[16,128,128]{2,1,0:T(8,128)S(1)} %collective-permute-done.5), channel_id=1, source_target_pairs={{0,480},{16,496},{32,0},{48,16},{64,32},{80,48},{96,64},{112,80},{... | collective-permute-start | bytes 3145736 | tf_op jit(solution)/shard_map/ppermute | solution.py:23
  111.9 117.6 %collective-permute-start.11 = (f32[16,128,128]{2,1,0:T(8,128)}, f32[16,128,128]{2,1,0:T(8,128)}, u32[]{:S(2)}, u32[]{:S(2)}) collective-permute-start(f32[16,128,128]{2,1,0:T(8,128)} %collective-permute-done.8), channel_id=1, source_target_pairs={{0,480},{16,496},{32,0},{48,16},{64,32},{80,48},{96,64},{112,80},{... | collective-permute-start | bytes 3145736 | tf_op jit(solution)/shard_map/ppermute | solution.py:23
  207.6 3.1 %copy-start.2 = (f32[8,128,128]{2,1,0:T(8,128)S(1)}, f32[8,128,128]{2,1,0:T(8,128)}, u32[]{:S(2)}) copy-start(f32[8,128,128]{2,1,0:T(8,128)} %get-tuple-element.43) | copy-start | bytes 1572868
  210.7 2.0 copy-start.1
  212.7 2.1 copy-start
  220.0 4.7 %copy-start.5 = (f32[32,128,128]{2,1,0:T(8,128)S(1)}, f32[32,128,128]{2,1,0:T(8,128)}, u32[]{:S(2)}) copy-start(f32[32,128,128]{2,1,0:T(8,128)} %gather_fusion.2) | copy-start | bytes 6291460
  224.8 2.4 copy-start.4
  224.8 2.4 copy-start.6
  229.5 3.4 %copy-start.3 = (f32[32,128,128]{2,1,0:T(8,128)S(1)}, f32[32,128,128]{2,1,0:T(8,128)}, u32[]{:S(2)}) copy-start(f32[32,128,128]{2,1,0:T(8,128)} %gather_fusion.6) | copy-start | bytes 6291460
Sparse Core Ops, SparseCore 0:
  71.6 135.9 all-reduce.3
where the time goes:
time: 245 us; the launch traced here: 244 us
  waiting for transfers between devices  126 us (51%)
  starting transfers between devices  47.7 us (19%)
  local copies, waits for them, and re-layouts  20.2 us (8%)
  matrix products  14 us (6%)
  blocking collectives  13.9 us (6%)
  between operations  13.9 us (6%)
  other arithmetic  8.89 us (4%)
    psum x1, waiting for transfers between devices, from_root(): return lax.psum(jnp.where(mine, x, jnp.zeros_like(x)), axis)  89.4 us
    ppermute x9, waiting for transfers between devices, shifted(): return lax.ppermute(value, axis, pairs)  35.3 us
    ppermute x9, starting transfers between devices, shifted(): return lax.ppermute(value, axis, pairs)  35.2 us
    dot_general x4, matrix products, section_product(): jnp.einsum('tqij,tqjk->tik', left, right, precision=lax.Precision.HIGHEST...  14 us
    psum x1, blocking collectives, from_root(): return lax.psum(jnp.where(mine, x, jnp.zeros_like(x)), axis)  13.9 us
    ppermute x3, starting transfers between devices, from_partner(): lax.ppermute(x, axis, [(i, i ^ 1 << bit) for i in range(lax.axis_size(axi...  12.4 us
    gather x4, local copies, waits for them, and re-layouts, section_product(): right = pair_vals[pair_slot]  9.31 us
    gather x4, local copies, waits for them, and re-layouts, section_product(): left = panel_vals[panel_slot] * weight[:, :, None, None]  9.18 us
  transfers between devices with their start and end apart: 13, of which 4 were waited for; matrix products, arithmetic and copies ran while one was open for 14% of the time, Pallas kernels for 0%

commit v1 on v0

--- a/solution.py
+++ b/solution.py
@@ -10,7 +10,7 @@
 
 def from_root(x, axis, root):
     mine = lax.axis_index(axis) == root
-    return lax.psum(jnp.where(mine, x, jnp.zeros_like(x)), axis)
+    return jnp.sum(lax.all_gather(jnp.where(mine, x, jnp.zeros_like(x)), axis), axis=0)
 
 
 def from_partner(x, axis, bit):

time: 245 us -> 309 us (1.26); the launches traced: 244 us -> 305 us
  blocking collectives: 13.9 us -> 138 us
  waiting for transfers between devices: 126 us -> 55.2 us
  other arithmetic: 8.89 us -> 22.1 us
    all_gather x0 -> x8, blocking collectives: none -> 138 us  [from_root(): lax.all_gather(jnp.where(mine, x, jnp.zeros_like(x)), axis)]
    psum x1 -> x0, waiting for transfers between devices: 89.4 us -> none  [from_root(): return lax.psum(jnp.where(mine, x, jnp.zeros_like(x)), axis)]
    ppermute x9, waiting for transfers between devices: 35.3 us -> 53.3 us  [shifted(): return lax.ppermute(value, axis, pairs)]
    reduce_sum x0 -> x12, other arithmetic: none -> 16.1 us  [from_root(): jnp.sum(lax.all_gather(jnp.where(mine, x, jnp.zeros_like(x)), axis), axis=0)]
    psum x1 -> x0, blocking collectives: 13.9 us -> none  [from_root(): return lax.psum(jnp.where(mine, x, jnp.zeros_like(x)), axis)]
  transfers between devices with their start and end apart: 13 -> 16, of which waited for: 4 -> 3; matrix products, arithmetic and copies ran while one was open for 14% -> 10% of each run, Pallas kernels for 0% -> 0%
where the time goes in v1:
time: 309 us; the launch traced here: 305 us
  blocking collectives  138 us (45%)
  waiting for transfers between devices  55.2 us (18%)
  starting transfers between devices  45.8 us (15%)
  other arithmetic  22.1 us (7%)
  local copies, waits for them, and re-layouts  17.7 us (6%)
  between operations  13.7 us (4%)
  matrix products  12.5 us (4%)
    all_gather x8, blocking collectives, from_root(): lax.all_gather(jnp.where(mine, x, jnp.zeros_like(x)), axis)  138 us
    ppermute x9, waiting for transfers between devices, shifted(): return lax.ppermute(value, axis, pairs)  53.3 us
    ppermute x9, starting transfers between devices, shifted(): return lax.ppermute(value, axis, pairs)  33.3 us
    reduce_sum x12, other arithmetic, from_root(): jnp.sum(lax.all_gather(jnp.where(mine, x, jnp.zeros_like(x)), axis), axis=0)  16.1 us
    dot_general x4, matrix products, section_product(): jnp.einsum('tqij,tqjk->tik', left, right, precision=lax.Precision.HIGHEST...  12.5 us
    ppermute x3, starting transfers between devices, from_partner(): lax.ppermute(x, axis, [(i, i ^ 1 << bit) for i in range(lax.axis_size(axi...  12.4 us
    gather x4, local copies, waits for them, and re-layouts, section_product(): left = panel_vals[panel_slot] * weight[:, :, None, None]  8.09 us
    gather x4, local copies, waits for them, and re-layouts, section_product(): right = pair_vals[pair_slot]  7.93 us
  transfers between devices with their start and end apart: 16, of which 3 were waited for; matrix products, arithmetic and copies ran while one was open for 10% of the time, Pallas kernels for 0%

profile of v1, /device:TPU:1, one launch (start us, length us, event | category | flops | bytes accessed | tf_op | source)
XLA Modules:
  0.0 305.2 jit_solution(10791978656289718815)
XLA Ops:
  6.5 2.5 broadcast_select_fusion
  9.1 0.7 all-gather.19.cloned.1.call-update
  9.8 0.7 all-gather.21.cloned.1.call-update
  10.6 0.5 all-gather.23.cloned.1.call-update
  11.1 5.7 %collective-permute-start.2 = (f32[8,128,128]{2,1,0:T(8,128)S(1)}, f32[8,128,128]{2,1,0:T(8,128)S(1)}, u32[]{:S(2)}, u32[]{:S(2)}) collective-permute-start(f32[8,128,128]{2,1,0:T(8,128)S(1)} %bitcast.84), channel_id=1, source_target_pairs={{0,16},{16,0},{32,48},{48,32},{64,80},{80,64},{96,112},{112,96},{1... | collective-permute-start | bytes 1572872 | tf_op jit(solution)/shard_map/ppermute | solution.py:17
  16.8 1.9 collective-permute-start
  18.7 4.9 %collective-permute-start.1 = (s32[8]{0:T(128)S(1)}, s32[8]{0:T(128)S(1)}, u32[]{:S(2)}, u32[]{:S(2)}) collective-permute-start(s32[8]{0:T(128)S(1)} %bitcast.87), channel_id=1, source_target_pairs={{0,16},{16,0},{32,48},{48,32},{64,80},{80,64},{96,112},{112,96},{1... | collective-permute-start | bytes 104 | tf_op jit(solution)/shard_map/ppermute | solution.py:17
  23.6 20.0 %all-gather.10 = s32[16,1,8]{2,1,0:T(1,128)S(1)} all-gather(s32[1,1,8]{2,1,0:T(1,128)S(1)} %get-tuple-element.56), channel_id=12, replica_groups=mesh['row'=32,'col'=16] {'col'}, dimensions={0}, use_global_device_ids=true | all-gather | bytes 544 | tf_op jit(solution)/shard_map/all_gather | solution.py:13
  43.6 17.2 %all-gather.1 = s32[16,1,8]{2,1,0:T(1,128)S(1)} all-gather(s32[1,1,8]{2,1,0:T(1,128)S(1)} %get-tuple-element.54), channel_id=3, replica_groups=mesh['row'=32,'col'=16] {'col'}, dimensions={0}, use_global_device_ids=true | all-gather | bytes 544 | tf_op jit(solution)/shard_map/all_gather | solution.py:13
  60.8 16.5 %all-gather.4 = s32[16,1,8]{2,1,0:T(1,128)S(1)} all-gather(s32[1,1,8]{2,1,0:T(1,128)S(1)} %get-tuple-element.55), channel_id=6, replica_groups=mesh['row'=32,'col'=16] {'col'}, dimensions={0}, use_global_device_ids=true | all-gather | bytes 544 | tf_op jit(solution)/shard_map/all_gather | solution.py:13
  77.4 17.1 %all-gather.7 = s32[16,1,8]{2,1,0:T(1,128)S(1)} all-gather(s32[1,1,8]{2,1,0:T(1,128)S(1)} %get-tuple-element.57), channel_id=9, replica_groups=mesh['row'=32,'col'=16] {'col'}, dimensions={0}, use_global_device_ids=true | all-gather | bytes 544 | tf_op jit(solution)/shard_map/all_gather | solution.py:13
  94.6 16.5 %all-gather.11 = s32[16,1,8]{2,1,0:T(1,128)S(1)} all-gather(s32[1,1,8]{2,1,0:T(1,128)S(1)} %get-tuple-element.60), channel_id=13, replica_groups=mesh['row'=32,'col'=16] {'col'}, dimensions={0}, use_global_device_ids=true | all-gather | bytes 544 | tf_op jit(solution)/shard_map/all_gather | solution.py:13
  111.1 17.1 %all-gather.5 = s32[16,1,8]{2,1,0:T(1,128)S(1)} all-gather(s32[1,1,8]{2,1,0:T(1,128)S(1)} %get-tuple-element.59), channel_id=7, replica_groups=mesh['row'=32,'col'=16] {'col'}, dimensions={0}, use_global_device_ids=true | all-gather | bytes 544 | tf_op jit(solution)/shard_map/all_gather | solution.py:13
  128.3 16.5 %all-gather.8 = s32[16,1,8]{2,1,0:T(1,128)S(1)} all-gather(s32[1,1,8]{2,1,0:T(1,128)S(1)} %get-tuple-element.61), channel_id=10, replica_groups=mesh['row'=32,'col'=16] {'col'}, dimensions={0}, use_global_device_ids=true | all-gather | bytes 544 | tf_op jit(solution)/shard_map/all_gather | solution.py:13
  144.8 17.1 %all-gather.2 = s32[16,1,8]{2,1,0:T(1,128)S(1)} all-gather(s32[1,1,8]{2,1,0:T(1,128)S(1)} %get-tuple-element.58), channel_id=4, replica_groups=mesh['row'=32,'col'=16] {'col'}, dimensions={0}, use_global_device_ids=true | all-gather | bytes 544 | tf_op jit(solution)/shard_map/all_gather | solution.py:13
  162.0 0.2 convert_reduce_fusion.8
  162.2 0.2 convert_reduce_fusion.10
  162.4 0.2 convert_reduce_fusion.9
  162.6 0.2 convert_reduce_fusion.11
  162.9 1.0 select_reduce_fusion.2
  164.0 0.1 reshape.685
  164.1 0.1 reshape.701
  164.2 0.1 copy.34
  164.5 0.1 reshape.733
  164.8 12.5 %collective-permute-start.4 = (s32[16]{0:T(128)S(1)}, s32[16]{0:T(128)S(1)}, u32[]{:S(2)}, u32[]{:S(2)}) collective-permute-start(s32[16]{0:T(128)S(1)} %pad_add_fusion.1), channel_id=1, source_target_pairs={{0,480},{16,496},{32,0},{48,16},{64,32},{80,48},{96,64},{112,80},{... | collective-permute-start | bytes 200 | tf_op jit(solution)/shard_map/ppermute | solution.py:23
  177.4 2.3 collective-permute-start.3
  179.7 3.1 %collective-permute-start.7 = (s32[16]{0:T(128)S(1)}, s32[16]{0:T(128)S(1)}, u32[]{:S(2)}, u32[]{:S(2)}) collective-permute-start(s32[16]{0:T(128)S(1)} %collective-permute-done.4), channel_id=1, source_target_pairs={{0,480},{16,496},{32,0},{48,16},{64,32},{80,48},{96,64},{112,80},{... | collective-permute-start | bytes 200 | tf_op jit(solution)/shard_map/ppermute | solution.py:23
  182.8 0.1 broadcast_select_fusion.5
  182.9 0.1 pad_maximum_fusion
  183.0 1.9 collective-permute-start.5
  184.9 2.5 collective-permute-start.6
  187.5 2.2 collective-permute-start.10
  189.6 18.2 %collective-permute-done.6 = s32[16]{0:T(128)S(1)} collective-permute-done((s32[16]{0:T(128)S(1)}, s32[16]{0:T(128)S(1)}, u32[]{:S(2)}, u32[]{:S(2)}) %collective-permute-start.6) | collective-permute-done | bytes 96 | tf_op jit(solution)/shard_map/ppermute | solution.py:23
  207.9 3.4 %collective-permute-start.9 = (s32[16]{0:T(128)S(1)}, s32[16]{0:T(128)S(1)}, u32[]{:S(2)}, u32[]{:S(2)}) collective-permute-start(s32[16]{0:T(128)S(1)} %collective-permute-done.6), channel_id=1, source_target_pairs={{0,480},{16,496},{32,0},{48,16},{64,32},{80,48},{96,64},{112,80},{... | collective-permute-start | bytes 200 | tf_op jit(solution)/shard_map/ppermute | solution.py:23
  211.4 0.3 convert_reduce_fusion.6
  211.7 1.9 collective-permute-start.8
  213.6 0.3 convert_reduce_fusion.4
  213.9 0.3 convert_reduce_fusion.2
  214.3 21.5 %collective-permute-done.8 = f32[16,128,128]{2,1,0:T(8,128)S(1)} collective-permute-done((f32[16,128,128]{2,1,0:T(8,128)S(1)}, f32[16,128,128]{2,1,0:T(8,128)S(1)}, u32[]{:S(2)}, u32[]{:S(2)}) %collective-permute-start.8) | collective-permute-done | bytes 1048608 | tf_op jit(solution)/shard_map/ppermute | solution.py:23
  235.7 3.5 %collective-permute-start.11 = (f32[16,128,128]{2,1,0:T(8,128)S(1)}, f32[16,128,128]{2,1,0:T(8,128)}, u32[]{:S(2)}, u32[]{:S(2)}) collective-permute-start(f32[16,128,128]{2,1,0:T(8,128)S(1)} %collective-permute-done.8), channel_id=1, source_target_pairs={{0,480},{16,496},{32,0},{48,16},{64,32},{80,48},{96,64},{112,80},{... | collective-permute-start | bytes 3145736 | tf_op jit(solution)/shard_map/ppermute | solution.py:23
  239.3 0.1 reshape.693
  239.6 0.1 reshape.709
  239.8 0.1 reshape.725
  240.0 0.3 convert_reduce_fusion
  240.3 0.1 copy.39
  240.4 0.1 reshape.741
  240.4 0.1 copy.38
  240.6 2.0 gather_fusion.1
  242.6 2.0 gather_fusion.3
  244.6 0.7 gather_fusion.5
  245.3 13.6 %collective-permute-done.11 = f32[16,128,128]{2,1,0:T(8,128)} collective-permute-done((f32[16,128,128]{2,1,0:T(8,128)S(1)}, f32[16,128,128]{2,1,0:T(8,128)}, u32[]{:S(2)}, u32[]{:S(2)}) %collective-permute-start.11) | collective-permute-done | bytes 1048608 | tf_op jit(solution)/shard_map/ppermute | solution.py:23
  258.9 3.2 %gather_fusion.7 = f32[32,128,128]{2,1,0:T(8,128)} fusion(f32[16,128,128]{2,1,0:T(8,128)} %collective-permute-done.11, s32[1024]{0:T(1024)S(1)} %pad_clamp_fusion), kind=kCustom, calls=%fused_computation.7 | custom fusion | bytes 4194432 | tf_op jit(solution)/shard_map/gather | solution.py:55
  262.1 4.0 %reduce_sum.340 = f32[8,128,128]{2,1,0:T(8,128)S(1)} reduce(f32[16,1,8,128,128]{4,3,2,1,0:T(8,128)} %all-gather.17.cloned.1.call-done, f32[]{:T(128)} %constant.84.clone.1), dimensions={0,1}, to_apply=%region_0.1 | reduce | flops 1966080 | bytes 8912900 | tf_op jit(solution)/shard_map/reduce_sum | solution.py:13
  266.1 2.1 gather_fusion
  268.2 3.9 %reduce_sum.351 = f32[8,128,128]{2,1,0:T(8,128)S(1)} reduce(f32[16,1,8,128,128]{4,3,2,1,0:T(8,128)} %all-gather.19.cloned.1.call-done, f32[]{:T(128)} %constant.84.clone.1), dimensions={0,1}, to_apply=%region_9.10 | reduce | flops 1966080 | bytes 8912900 | tf_op jit(solution)/shard_map/reduce_sum | solution.py:13
  272.1 2.0 gather_fusion.2
  274.1 3.9 %reduce_sum.362 = f32[8,128,128]{2,1,0:T(8,128)S(1)} reduce(f32[16,1,8,128,128]{4,3,2,1,0:T(8,128)} %all-gather.21.cloned.1.call-done, f32[]{:T(128)} %constant.84.clone.1), dimensions={0,1}, to_apply=%region_18.19 | reduce | flops 1966080 | bytes 8912900 | tf_op jit(solution)/shard_map/reduce_sum | solution.py:13
  278.0 2.0 gather_fusion.4
  280.1 3.9 %reduce_sum.373 = f32[8,128,128]{2,1,0:T(8,128)S(1)} reduce(f32[16,1,8,128,128]{4,3,2,1,0:T(8,128)} %all-gather.23.cloned.1.call-done, f32[]{:T(128)} %constant.84.clone.1), dimensions={0,1}, to_apply=%region_27.28 | reduce | flops 1966080 | bytes 8912900 | tf_op jit(solution)/shard_map/reduce_sum | solution.py:13
  284.0 2.0 gather_fusion.6
  286.0 4.7 %fusion.8 = f32[8,128,128]{2,1,0:T(8,128)S(1)} fusion(f32[8,4,128,128]{3,2,1,0:T(8,128)} %bitcast.82, f32[8,4,128,128]{3,2,1,0:T(8,128)} %bitcast.83, f32[8,4]{1,0:T(8,128)S(1)} %copy.29), kind=kOutput, calls=%fused_computation.16 | convolution fusion | flops 805830656 | bytes 4718720 | tf_op jit(solution)/shard_map/tqij,tqjk->tik/dot_general | solution.py:56
  290.7 2.4 fusion.29
  293.2 2.4 fusion.26
  295.6 3.1 %fusion.23 = f32[1,1,8,128,128]{4,3,2,1,0:T(8,128)} fusion(f32[8,128,128]{2,1,0:T(8,128)S(1)} %fusion.26, f32[8,4,128,128]{3,2,1,0:T(8,128)S(1)} %bitcast.77, f32[8,4,128,128]{3,2,1,0:T(8,128)S(1)} %bitcast.81, f32[8,4]{1,0:T(8,128)S(1)} %copy.38), kind=kOutput, calls=%fused_computation.21 | convolution fusion | flops 805961728 | bytes 5243008 | tf_op jit(solution)/shard_map/tqij,tqjk->tik/dot_general | solution.py:56
  (94 shorter events, 1.8 us)
Async XLA Ops:
  6.5 255.6 %all-gather.17.cloned.1.call-start = ((), (), s32[]{:S(2)}) async-start(), calls=%async_computation | async-start | bytes 8912896 | tf_op jit(solution)/shard_map/all_gather | solution.py:13
  6.5 4.5 %copy-start.5 = (f32[1,1,8,128,128]{4,3,2,1,0:T(8,128)S(1)}, f32[1,1,8,128,128]{4,3,2,1,0:T(8,128)}, u32[]{:S(2)}) copy-start(f32[1,1,8,128,128]{4,3,2,1,0:T(8,128)} %param.3) | copy-start | bytes 1572868
  6.5 10.2 %copy-start.6 = (s32[1,1,8]{2,1,0:T(1,128)S(1)}, s32[1,1,8]{2,1,0:T(1,128)}, u32[]{:S(2)}) copy-start(s32[1,1,8]{2,1,0:T(1,128)} %param.4) | copy-start | bytes 100
  6.5 12.2 %copy-start.7 = (s32[1,1,8]{2,1,0:T(1,128)S(1)}, s32[1,1,8]{2,1,0:T(1,128)}, u32[]{:S(2)}) copy-start(s32[1,1,8]{2,1,0:T(1,128)} %param.5) | copy-start | bytes 100
  9.0 259.1 %all-gather.19.cloned.1.call-start = ((), (), s32[]{:S(2)}) async-start(), calls=%async_computation.1 | async-start | bytes 8912896 | tf_op jit(solution)/shard_map/all_gather | solution.py:13
  9.8 264.3 %all-gather.21.cloned.1.call-start = ((), (), s32[]{:S(2)}) async-start(), calls=%async_computation.2 | async-start | bytes 8912896 | tf_op jit(solution)/shard_map/all_gather | solution.py:13
  10.5 269.6 %all-gather.23.cloned.1.call-start = ((), (), s32[]{:S(2)}) async-start(), calls=%async_computation.3 | async-start | bytes 8912896 | tf_op jit(solution)/shard_map/all_gather | solution.py:13
  11.1 171.7 %collective-permute-start.2 = (f32[8,128,128]{2,1,0:T(8,128)S(1)}, f32[8,128,128]{2,1,0:T(8,128)S(1)}, u32[]{:S(2)}, u32[]{:S(2)}) collective-permute-start(f32[8,128,128]{2,1,0:T(8,128)S(1)} %bitcast.84), channel_id=1, source_target_pairs={{0,16},{16,0},{32,48},{48,32},{64,80},{80,64},{96,112},{112,96},{1... | collective-permute-start | bytes 1572872 | tf_op jit(solution)/shard_map/ppermute | solution.py:17
  16.8 160.5 %collective-permute-start = (s32[8]{0:T(128)S(1)}, s32[8]{0:T(128)S(1)}, u32[]{:S(2)}, u32[]{:S(2)}) collective-permute-start(s32[8]{0:T(128)S(1)} %bitcast.85), channel_id=1, source_target_pairs={{0,16},{16,0},{32,48},{48,32},{64,80},{80,64},{96,112},{112,96},{1... | collective-permute-start | bytes 104 | tf_op jit(solution)/shard_map/ppermute | solution.py:17
  18.7 146.0 %collective-permute-start.1 = (s32[8]{0:T(128)S(1)}, s32[8]{0:T(128)S(1)}, u32[]{:S(2)}, u32[]{:S(2)}) collective-permute-start(s32[8]{0:T(128)S(1)} %bitcast.87), channel_id=1, source_target_pairs={{0,16},{16,0},{32,48},{48,32},{64,80},{80,64},{96,112},{112,96},{1... | collective-permute-start | bytes 104 | tf_op jit(solution)/shard_map/ppermute | solution.py:17
  164.8 14.9 %collective-permute-start.4 = (s32[16]{0:T(128)S(1)}, s32[16]{0:T(128)S(1)}, u32[]{:S(2)}, u32[]{:S(2)}) collective-permute-start(s32[16]{0:T(128)S(1)} %pad_add_fusion.1), channel_id=1, source_target_pairs={{0,480},{16,496},{32,0},{48,16},{64,32},{80,48},{96,64},{112,80},{... | collective-permute-start | bytes 200 | tf_op jit(solution)/shard_map/ppermute | solution.py:23
  177.4 7.5 %collective-permute-start.3 = (s32[16]{0:T(128)S(1)}, s32[16]{0:T(128)S(1)}, u32[]{:S(2)}, u32[]{:S(2)}) collective-permute-start(s32[16]{0:T(128)S(1)} %get-tuple-element.35), channel_id=1, source_target_pairs={{0,480},{16,496},{32,0},{48,16},{64,32},{80,48},{96,64},{112,80},{... | collective-permute-start | bytes 200 | tf_op jit(solution)/shard_map/ppermute | solution.py:23
  179.7 7.8 %collective-permute-start.7 = (s32[16]{0:T(128)S(1)}, s32[16]{0:T(128)S(1)}, u32[]{:S(2)}, u32[]{:S(2)}) collective-permute-start(s32[16]{0:T(128)S(1)} %collective-permute-done.4), channel_id=1, source_target_pairs={{0,480},{16,496},{32,0},{48,16},{64,32},{80,48},{96,64},{112,80},{... | collective-permute-start | bytes 200 | tf_op jit(solution)/shard_map/ppermute | solution.py:23
  183.0 28.7 %collective-permute-start.5 = (f32[16,128,128]{2,1,0:T(8,128)S(1)}, f32[16,128,128]{2,1,0:T(8,128)S(1)}, u32[]{:S(2)}, u32[]{:S(2)}) collective-permute-start(f32[16,128,128]{2,1,0:T(8,128)S(1)} %pad_maximum_fusion), channel_id=1, source_target_pairs={{0,480},{16,496},{32,0},{48,16},{64,32},{80,48},{96,64},{112,80},{... | collective-permute-start | bytes 3145736 | tf_op jit(solution)/shard_map/ppermute | solution.py:23
  184.9 23.0 %collective-permute-start.6 = (s32[16]{0:T(128)S(1)}, s32[16]{0:T(128)S(1)}, u32[]{:S(2)}, u32[]{:S(2)}) collective-permute-start(s32[16]{0:T(128)S(1)} %collective-permute-done.3), channel_id=1, source_target_pairs={{0,480},{16,496},{32,0},{48,16},{64,32},{80,48},{96,64},{112,80},{... | collective-permute-start | bytes 200 | tf_op jit(solution)/shard_map/ppermute | solution.py:23
  187.5 23.8 %collective-permute-start.10 = (s32[16]{0:T(128)S(1)}, s32[16]{0:T(128)S(1)}, u32[]{:S(2)}, u32[]{:S(2)}) collective-permute-start(s32[16]{0:T(128)S(1)} %collective-permute-done.7), channel_id=1, source_target_pairs={{0,480},{16,496},{32,0},{48,16},{64,32},{80,48},{96,64},{112,80},{... | collective-permute-start | bytes 200 | tf_op jit(solution)/shard_map/ppermute | solution.py:23
  207.9 31.3 %collective-permute-start.9 = (s32[16]{0:T(128)S(1)}, s32[16]{0:T(128)S(1)}, u32[]{:S(2)}, u32[]{:S(2)}) collective-permute-start(s32[16]{0:T(128)S(1)} %collective-permute-done.6), channel_id=1, source_target_pairs={{0,480},{16,496},{32,0},{48,16},{64,32},{80,48},{96,64},{112,80},{... | collective-permute-start | bytes 200 | tf_op jit(solution)/shard_map/ppermute | solution.py:23
  211.7 24.0 %collective-permute-start.8 = (f32[16,128,128]{2,1,0:T(8,128)S(1)}, f32[16,128,128]{2,1,0:T(8,128)S(1)}, u32[]{:S(2)}, u32[]{:S(2)}) collective-permute-start(f32[16,128,128]{2,1,0:T(8,128)S(1)} %collective-permute-done.5), channel_id=1, source_target_pairs={{0,480},{16,496},{32,0},{48,16},{64,32},{80,48},{96,64},{112,80},{... | collective-permute-start | bytes 3145736 | tf_op jit(solution)/shard_map/ppermute | solution.py:23
  235.7 23.2 %collective-permute-start.11 = (f32[16,128,128]{2,1,0:T(8,128)S(1)}, f32[16,128,128]{2,1,0:T(8,128)}, u32[]{:S(2)}, u32[]{:S(2)}) collective-permute-start(f32[16,128,128]{2,1,0:T(8,128)S(1)} %collective-permute-done.8), channel_id=1, source_target_pairs={{0,480},{16,496},{32,0},{48,16},{64,32},{80,48},{96,64},{112,80},{... | collective-permute-start | bytes 3145736 | tf_op jit(solution)/shard_map/ppermute | solution.py:23
  286.0 4.7 %copy-start.1 = (f32[32,128,128]{2,1,0:T(8,128)S(1)}, f32[32,128,128]{2,1,0:T(8,128)}, u32[]{:S(2)}) copy-start(f32[32,128,128]{2,1,0:T(8,128)} %gather_fusion.3) | copy-start | bytes 6291460
  286.0 4.7 %copy-start.2 = (f32[32,128,128]{2,1,0:T(8,128)S(1)}, f32[32,128,128]{2,1,0:T(8,128)}, u32[]{:S(2)}) copy-start(f32[32,128,128]{2,1,0:T(8,128)} %gather_fusion.2) | copy-start | bytes 6291460
  290.7 2.4 copy-start.3
  293.1 2.4 copy-start
  293.1 2.4 copy-start.4
Sparse Core Ops, SparseCore 0:
  9.5 65.6 all-gather.16
  77.3 60.8 all-gather.18
  140.4 60.6 all-gather.20
  203.0 60.7 all-gather.22
